TPU v7x, 32 devices: a whole 2x2x4 slice. The times are simulated.
32 devices in a mesh: dp: 16 (over z, x, core), group: 2 (over y).
Axes of the slice: x: 2, y: 2, z: 4, core: 2. Of those that a mesh axis runs over, the one named last changes fastest.
Arguments:
- queries: bfloat16 [4096, 256], P('dp'), may hold values from -110 to 110
- item_features: bfloat16 [4096, 2048], P('dp', 'group'), may hold values from -6 to 6
- corpus: bfloat16 [32768, 2048], P('dp', 'group'), may hold values from -6 to 6
- sample_ids: int32 [16384], P('dp'), may hold values from 0 to 2047
- sample_shift: bfloat16 [16384], P('dp'), may hold values from -2 to 2
- w1: bfloat16 [2048, 1024], P(None, 'group'), may hold values from -0.125 to 0.125
- w2: bfloat16 [1024, 256], P('group'), may hold values from -0.1875 to 0.1875
Outputs:
- query_loss: float32 [4096], P(('dp', 'group'))
- grad_query: float32 [4096, 256], P(('dp', 'group'))
- grad_w1: float32 [2048, 1024], P(None, 'group')
- grad_w2: float32 [1024, 256], P('group')
Inputs may be any that keep to these rules, and one draw needn't show every extreme that they name: sample_ids[k] is a row of the corpus block of the dp index that holds position k.
All inputs are finite; a program needn't handle non-finite values.
Results may differ from a plain program's by a relative error of at most 0.02.
The roundings to bfloat16 on the way count: a program that leaves them out, or rounds other values in their place, can miss the bound.
Values may be sent and summed in bfloat16 or wider, within the bound.
A program may use at most 128 MiB of HBM per device.

v0:
```python
import jax
import jax.numpy as jnp
from jax import lax
from jax.sharding import PartitionSpec as P


def alternate(head_part, tail_part, groups):
    emb_cols = head_part.shape[1]
    joined = jnp.concatenate(
        [head_part.reshape(groups, -1, emb_cols), tail_part.reshape(groups, -1, emb_cols)], 1
    )
    return joined.reshape(-1, emb_cols)


def per_device(queries, item_features, corpus, sample_ids, sample_shift, w1, w2):
    groups = lax.axis_size("group")
    member = lax.axis_index("group")
    query_rows, emb_width = queries.shape
    quota_rows = query_rows // groups
    neg_rows = sample_ids.shape[0] // groups
    score_scale = emb_width ** (-0.5)
    block_rows = 256
    steps_count = query_rows // block_rows
    picked = jnp.take(corpus, sample_ids, axis=0)
    features_local = alternate(item_features, picked, groups)
    gathered = lax.all_gather(features_local, "group", axis=1, tiled=True)
    pre_act = jnp.dot(gathered, w1, preferred_element_type=jnp.float32)
    hidden = jnp.maximum(pre_act, 0.0).astype(jnp.bfloat16)
    partial_embed = jnp.dot(hidden, w2, preferred_element_type=jnp.float32)
    embedded = lax.psum_scatter(partial_embed, "group", scatter_dimension=0, tiled=True)
    inverse = lax.rsqrt(jnp.mean(embedded * embedded, -1, keepdims=True) + 1e-06)
    normed = (embedded * inverse).astype(jnp.bfloat16)
    shift_own = lax.dynamic_slice_in_dim(sample_shift, member * neg_rows, neg_rows)
    bias_own = jnp.concatenate([jnp.zeros((quota_rows,), jnp.bfloat16), -shift_own])
    stashed, bias_all = (
        lax.all_gather(normed, "dp", axis=0, tiled=True),
        lax.all_gather(bias_own, "dp", axis=0, tiled=True),
    )
    bias_wide = bias_all.astype(jnp.float32)
    query_blocks = queries.reshape(steps_count, block_rows, emb_width)

    def score_block(query_blk):
        return (
            score_scale
            * jnp.einsum("qe,ce->qc", query_blk, stashed, preferred_element_type=jnp.float32)
            + bias_wide
        )

    def row_stats(query_blk):
        logits = score_block(query_blk)
        highest = jnp.max(logits, -1)
        return (highest, jnp.sum(jnp.exp(logits - highest[:, None]), -1))

    highest, row_sum = lax.map(row_stats, query_blocks)
    highest = highest.reshape(query_rows)
    row_sum = row_sum.reshape(query_rows)
    largest = lax.pmax(highest, "group")
    row_sum = lax.psum(row_sum * jnp.exp(highest - largest), "group")
    highest = largest
    log_total = highest + jnp.log(row_sum)
    query_own = lax.dynamic_slice_in_dim(queries, member * quota_rows, quota_rows)
    positive_own = normed[:quota_rows].astype(jnp.float32)
    positive = score_scale * jnp.sum(query_own.astype(jnp.float32) * positive_own, -1)
    query_loss = lax.dynamic_slice_in_dim(log_total, member * quota_rows, quota_rows) - positive
    total_blocks = log_total.reshape(steps_count, block_rows)

    def softmax_block(query_blk, total_blk):
        return jnp.exp(score_block(query_blk) - total_blk[:, None]).astype(jnp.bfloat16)

    def accumulate(grad_acc, inputs):
        query_blk, total_blk = inputs
        softmax = softmax_block(query_blk, total_blk)
        grad_acc = grad_acc + jnp.einsum(
            "qc,qe->ce", softmax, query_blk, preferred_element_type=jnp.float32
        )
        return (grad_acc, jnp.dot(softmax, stashed, preferred_element_type=jnp.float32))

    grad_acc, grad_blocks = lax.scan(
        accumulate, jnp.zeros(stashed.shape, jnp.float32), (query_blocks, total_blocks)
    )
    grad_hat = lax.psum_scatter(grad_acc, "dp", scatter_dimension=0, tiled=True)
    query_sum = lax.psum_scatter(
        grad_blocks.reshape(query_rows, emb_width), "group", scatter_dimension=0, tiled=True
    )
    grad_query = score_scale * (query_sum - positive_own)
    target = jnp.concatenate(
        [query_own.astype(jnp.float32), jnp.zeros((neg_rows, emb_width), jnp.float32)], 0
    )
    grad_normed = score_scale * (grad_hat - target)
    along = jnp.sum(grad_normed * embedded, -1, keepdims=True)
    grad_embed = inverse * grad_normed - inverse**3 * embedded * along / emb_width
    grad_back = lax.all_gather(grad_embed.astype(jnp.bfloat16), "group", axis=0, tiled=True)
    grad_pre = jnp.where(
        pre_act > 0, jnp.dot(grad_back, w2.T, preferred_element_type=jnp.float32), 0.0
    ).astype(jnp.bfloat16)
    grad_w2 = jnp.einsum("rh,re->he", hidden, grad_back, preferred_element_type=jnp.float32)
    grad_w1 = jnp.einsum("rf,rh->fh", gathered, grad_pre, preferred_element_type=jnp.float32)
    grad_w1, grad_w2 = lax.psum((grad_w1, grad_w2), "dp")
    return (query_loss, grad_query, grad_w1, grad_w2)


def solution(mesh):
    in_specs = (
        P("dp", None),
        P("dp", "group"),
        P("dp", "group"),
        P("dp"),
        P("dp"),
        P(None, "group"),
        P("group", None),
    )
    out_specs = (P(("dp", "group")), P(("dp", "group"), None), P(None, "group"), P("group", None))
    return jax.shard_map(
        per_device, mesh=mesh, in_specs=in_specs, out_specs=out_specs, check_vma=False
    )
```

profile of v0, /device:TPU:0, one launch (start us, length us, event | category | flops | bytes accessed | tf_op | source)
XLA Modules:
  0.0 489.6 jit_solution(1353273792064433591)
XLA Ops:
  7.2 0.0 copy-start
  7.2 0.0 all-gather.4.cloned.1.call-start
  7.2 0.8 fusion.9
  8.1 0.7 compare_and_fusion
  8.8 8.7 %gather_fusion = bf16[1024,1024]{1,0:T(8,128)(2,1)} fusion(bf16[2048,1024]{1,0:T(8,128)(2,1)} %param.9, s32[1024]{0:T(1024)S(1)} %fusion.9), kind=kCustom, calls=%fused_computation | custom fusion | bytes 4198400 | tf_op jit(solution)/shard_map/jit(_take)/gather | solution.py:24
  17.5 0.0 copy-start.4
  17.5 1.9 broadcast_select_fusion
  19.4 0.0 copy-done.4
  19.4 1.7 pad_maximum_fusion
  21.2 0.0 all-gather.4.cloned.1.call-update
  21.2 0.0 copy-start.6
  21.2 0.0 reduce-scatter.4.cloned.1.call-start
  21.2 71.4 %all-gather.4.cloned.1.call-done = bf16[1280,2048]{1,0:T(8,128)(2,1)} async-done(((bf16[1280,1024]{1,0:T(8,128)(2,1)}), bf16[1280,2048]{1,0:T(8,128)(2,1)}) %all-gather.4.cloned.1.call-update) | async-done | bytes 5242896 | tf_op jit(solution)/shard_map/all_gather | solution.py:26
  92.6 0.0 copy-done
  92.6 4.8 fusion.14
  97.4 0.0 copy-start.2
  97.4 1.5 copy-done.2
  98.9 0.0 copy-done.6
  98.9 0.0 copy-start.7
  98.9 0.0 copy-start.3
  98.9 1.6 fusion.6
  100.4 0.0 reduce-scatter.4.cloned.1.call-update
  100.5 0.0 all-gather.6.cloned.1.call-start
  100.5 23.3 %reduce-scatter.4.cloned.1.call-done = f32[640,256]{1,0:T(8,128)} async-done(((f32[1280,256]{1,0:T(8,128)}), f32[640,256]{1,0:T(8,128)}) %reduce-scatter.4.cloned.1.call-update) | async-done | bytes 655376 | tf_op jit(solution)/shard_map/reduce_scatter | solution.py:30
  123.8 1.3 multiply_reduce_fusion.1
  125.1 2.0 multiply_convert_fusion
  127.1 0.0 all-gather.6.cloned.1.call-update
  127.1 0.0 reduce-scatter.8.cloned.1.call-start
  127.1 0.0 copy-done.7
  127.2 0.1 dynamic-slice_negate_fusion
  127.2 21.6 %all-gather = bf16[16,1,640]{2,1,0:T(2,128)(2,1)S(1)} all-gather(bf16[1,1,640]{2,1,0:T(2,128)(2,1)S(1)} %reshape.68), channel_id=1, replica_groups=mesh['dp'=16,'group'=2] {'dp'}, dimensions={0}, use_global_device_ids=true | all-gather | bytes 21760 | tf_op jit(solution)/shard_map/all_gather | solution.py:37
  148.8 34.4 %all-gather.6.cloned.1.call-done = bf16[10240,256]{1,0:T(8,128)(2,1)} async-done(((bf16[640,256]{1,0:T(8,128)(2,1)}), bf16[10240,256]{1,0:T(8,128)(2,1)}) %all-gather.6.cloned.1.call-update) | async-done | bytes 5242896 | tf_op jit(solution)/shard_map/all_gather | solution.py:36
  183.3 0.0 copy-done.3
  183.3 6.6 %fusion.13 = (f32[256]{0:T(256)S(1)}, f32[10240,256]{1,0:T(8,128)}) fusion(f32[10240]{0:T(1024)S(1)} %bitcast.18, bf16[10240,256]{1,0:T(8,128)(2,1)} %all-gather.6.cloned.1.call-done, bf16[256,256]{1,0:T(8,128)(2,1)S(1)} %copy-done.3), kind=kOutput, calls=%fused_computation.38 | convolution fusion | flops 1350041344 | bytes 15901696 | tf_op jit(solution)/shard_map/while/body/eval_jaxpr/qe,ce->qc/dot_general | solution.py:45
  189.9 4.9 %pmax.7 = f32[256]{0:T(256)S(1)} all-reduce(f32[256]{0:T(256)S(1)} %get-tuple-element.43), channel_id=1, replica_groups=mesh['dp'=16,'group'=2] {'group'}, use_global_device_ids=true, to_apply=%region_3.4 | all-reduce | flops 256 | bytes 2048 | tf_op jit(solution)/shard_map/pmax | solution.py:57
  194.8 5.2 %exponential_reduce_fusion = f32[256]{0:T(256)S(1)} fusion(f32[10240,256]{1,0:T(8,128)} %get-tuple-element.44, f32[256]{0:T(256)S(1)} %get-tuple-element.43), kind=kLoop, calls=%fused_computation.4 | loop fusion | flops 5242624 | bytes 10487808 | tf_op jit(solution)/shard_map/while/body/eval_jaxpr/reduce_sum | solution.py:52
  200.0 4.9 %psum.21 = f32[256]{0:T(256)S(1)} all-reduce(f32[256]{0:T(256)S(1)} %exponential_multiply_fusion), channel_id=1, replica_groups=mesh['dp'=16,'group'=2] {'group'}, use_global_device_ids=true, to_apply=%region_5.6 | all-reduce | flops 256 | bytes 2048 | tf_op jit(solution)/shard_map/psum | solution.py:58
  205.0 9.5 %fusion.3 = f32[10240,256]{1,0:T(8,128)} fusion(bf16[256,256]{1,0:T(8,128)(2,1)S(1)} %copy-done.3, f32[10240,256]{1,0:T(8,128)} %get-tuple-element.44, f32[256]{0:T(256)S(1)} %log_add_fusion), kind=kOutput, calls=%fused_computation.11 | convolution fusion | flops 1347420160 | bytes 21103616 | tf_op jit(solution)/shard_map/while/body/eval_jaxpr/qc,qe->ce/dot_general | solution.py:73
  214.5 0.0 reduce-scatter.8.cloned.1.call-update
  214.5 0.0 reduce-scatter.6.cloned.1.call-start
  214.6 0.0 copy-start.1
  214.6 8.4 %fusion.2 = f32[256,256]{1,0:T(8,128)} fusion(bf16[10240,256]{1,0:T(8,128)(2,1)} %all-gather.6.cloned.1.call-done, f32[10240,256]{1,0:T(8,128)} %get-tuple-element.44, f32[256]{0:T(256)S(1)} %log_add_fusion), kind=kOutput, calls=%fused_computation.10 | convolution fusion | flops 1347420160 | bytes 15991808 | tf_op jit(solution)/shard_map/while/body/eval_jaxpr/dot_general | solution.py:76
  223.0 0.0 reduce-scatter.6.cloned.1.call-update
  223.0 0.0 all-reduce.5.cloned.1.call-start
  223.1 109.3 %reduce-scatter.8.cloned.1.call-done = f32[640,256]{1,0:T(8,128)} async-done(((f32[10240,256]{1,0:T(8,128)}), f32[640,256]{1,0:T(8,128)}) %reduce-scatter.8.cloned.1.call-update) | async-done | bytes 655376 | tf_op jit(solution)/shard_map/reduce_scatter | solution.py:81
  332.3 0.0 copy-done.1
  332.3 1.3 multiply_reduce_fusion
  333.6 1.4 subtract_convert_fusion
  335.0 13.0 %all_gather.15 = bf16[1280,256]{1,0:T(8,128)(2,1)S(1)} all-gather(bf16[640,256]{1,0:T(8,128)(2,1)S(1)} %subtract_convert_fusion), channel_id=1, replica_groups=mesh['dp'=16,'group'=2] {'group'}, dimensions={0}, use_global_device_ids=true | all-gather | bytes 983040 | tf_op jit(solution)/shard_map/all_gather | solution.py:92
  348.0 8.6 %fusion.4 = f32[2048,512]{1,0:T(8,128)} fusion(bf16[1280,2048]{1,0:T(8,128)(2,1)} %all-gather.4.cloned.1.call-done, bf16[1280,256]{1,0:T(8,128)(2,1)S(1)} %all_gather.15, bf16[512,256]{1,0:T(8,128)(2,1)S(1)} %copy-done.6, f32[1280,512]{1,0:T(8,128)} %copy-done.2), kind=kOutput, calls=%fused_computation.12 | convolution fusion | flops 3021864960 | bytes 12976128 | tf_op jit(solution)/shard_map/rf,rh->fh/dot_general | solution.py:97
  356.7 3.1 fusion.5
  359.7 0.0 all-reduce.5.cloned.1.call-update
  359.8 0.0 reduce-scatter.6.cloned.1.call-done
  359.8 1.6 fusion.8
  361.4 0.6 multiply_subtract_fusion
  362.0 115.3 %all-reduce.5.cloned.1.call-done = (f32[2048,512]{1,0:T(8,128)}, f32[512,256]{1,0:T(8,128)}) async-done(((f32[2048,512]{1,0:T(8,128)}, f32[512,256]{1,0:T(8,128)}), (f32[2048,512]{1,0:T(8,128)}, f32[512,256]{1,0:T(8,128)})) %all-reduce.5.cloned.1.call-update) | async-done | bytes 4718608 | tf_op jit(solution)/shard_map/psum | solution.py:98
  477.2 0.0 copy-start.5
  477.2 4.7 copy.13
  481.9 0.0 copy-done.5
  481.9 0.8 copy.14
  (8 shorter events, 0.1 us)
Async XLA Ops:
  7.2 85.4 %copy-start = (bf16[2048,512]{1,0:T(8,128)(2,1)S(1)}, bf16[2048,512]{1,0:T(8,128)(2,1)}, u32[]{:S(2)}) copy-start(bf16[2048,512]{1,0:T(8,128)(2,1)} %param.12) | copy-start | bytes 6291460
  7.2 85.4 %all-gather.4.cloned.1.call-start = ((), (), s32[]{:S(2)}) async-start(), calls=%async_computation.3 | async-start | bytes 7864320 | tf_op jit(solution)/shard_map/all_gather | solution.py:26
  17.5 1.9 copy-start.4
  21.2 77.7 %copy-start.6 = (bf16[512,256]{1,0:T(8,128)(2,1)S(1)}, bf16[512,256]{1,0:T(8,128)(2,1)}, u32[]{:S(2)}) copy-start(bf16[512,256]{1,0:T(8,128)(2,1)} %param.13) | copy-start | bytes 786436
  21.2 102.6 %reduce-scatter.4.cloned.1.call-start = ((), (), s32[]{:S(2)}) async-start(), calls=%async_computation.4 | async-start | bytes 1966080 | tf_op jit(solution)/shard_map/reduce_scatter | solution.py:30
  97.4 1.5 copy-start.2
  98.9 28.3 %copy-start.7 = (bf16[1024]{0:T(1024)(128)(2,1)S(1)}, bf16[1024]{0:T(1024)(128)(2,1)}, u32[]{:S(2)}) copy-start(bf16[1024]{0:T(1024)(128)(2,1)} %param.11) | copy-start | bytes 6148
  98.9 84.4 %copy-start.3 = (bf16[256,256]{1,0:T(8,128)(2,1)S(1)}, bf16[256,256]{1,0:T(8,128)(2,1)}, u32[]{:S(2)}) copy-start(bf16[256,256]{1,0:T(8,128)(2,1)} %param.7) | copy-start | bytes 393220
  100.5 82.8 %all-gather.6.cloned.1.call-start = ((), (), s32[]{:S(2)}) async-start(), calls=%async_computation.5 | async-start | bytes 5570560 | tf_op jit(solution)/shard_map/all_gather | solution.py:36
  127.1 205.3 %reduce-scatter.8.cloned.1.call-start = ((), (), s32[]{:S(2)}) async-start(), calls=%async_computation.7 | async-start | bytes 11141120 | tf_op jit(solution)/shard_map/reduce_scatter | solution.py:81
  214.5 145.3 %reduce-scatter.6.cloned.1.call-start = ((), (), s32[]{:S(2)}) async-start(), calls=%async_computation.6 | async-start | bytes 393216 | tf_op jit(solution)/shard_map/reduce_scatter | solution.py:82
  214.6 117.7 %copy-start.1 = (f32[640,256]{1,0:T(8,128)S(1)}, f32[640,256]{1,0:T(8,128)}, u32[]{:S(2)}) copy-start(f32[640,256]{1,0:T(8,128)} %reduce-scatter.4.cloned.1.call-done) | copy-start | bytes 1966084
  223.0 254.2 %all-reduce.5.cloned.1.call-start = ((), (), s32[]{:S(2)}) async-start(), calls=%async_computation.8 | async-start | bytes 9437184 | tf_op jit(solution)/shard_map/psum | solution.py:98
  477.2 4.7 copy-start.5
Sparse Core Ops, SparseCore 0:
  21.3 71.2 all-gather.3
  100.6 23.1 reduce-scatter.3
  127.2 56.0 all-gather.5
  214.6 117.6 reduce-scatter.7
  334.5 13.7 reduce-scatter.5
  359.9 117.3 all-reduce.4
where the time goes:
time: 490 us
  waiting for transfers between devices  354 us (72%)
  blocking collectives  44.4 us (9%)
  matrix products  42.6 us (9%)
  other arithmetic  18.6 us (4%)
  local copies, waits for them, and re-layouts  15.8 us (3%)
  between operations  14.2 us (3%)
    psum x1, waiting for transfers between devices, per_device(): grad_w1, grad_w2 = lax.psum((grad_w1, grad_w2), 'dp')  115 us
    reduce_scatter x1, waiting for transfers between devices, per_device(): grad_hat = lax.psum_scatter(grad_acc, 'dp', scatter_dimension=0, tiled=True)  109 us
    all_gather x1, waiting for transfers between devices, per_device(): gathered = lax.all_gather(features_local, 'group', axis=1, tiled=True)  71.4 us
    all_gather x1, waiting for transfers between devices, per_device(): lax.all_gather(normed, 'dp', axis=0, tiled=True)  34.4 us
    reduce_scatter x1, waiting for transfers between devices, per_device(): lax.psum_scatter(partial_embed, 'group', scatter_dimension=0, tiled=True)  23.3 us
    all_gather x1, blocking collectives, per_device(): lax.all_gather(bias_own, 'dp', axis=0, tiled=True)  21.6 us
    all_gather x1, blocking collectives, per_device(): lax.all_gather(grad_embed.astype(jnp.bfloat16), 'group', axis=0, tiled=True)  13 us
  transfers between devices with their start and end apart: 6, of which 5 were waited for; matrix products, arithmetic and copies ran while one was open for 5% of the time, Pallas kernels for 0%

commit v1 on v0

--- a/solution.py
+++ b/solution.py
@@ -2,6 +2,24 @@
 import jax.numpy as jnp
 from jax import lax
 from jax.sharding import PartitionSpec as P
+
+
+def laid_out(blocks, dim):
+    blocks = jnp.moveaxis(blocks, 0, dim)
+    shape = blocks.shape
+    return blocks.reshape(*shape[:dim], shape[dim] * shape[dim + 1], *shape[dim + 2 :])
+
+
+def doubled(value, axis):
+    count = lax.axis_size(axis)
+    blocks = value[None]
+    for level in range(count.bit_length() - 1):
+        stride = 1 << level
+        theirs = lax.ppermute(blocks, axis, [(i, i ^ stride) for i in range(count)])
+        both = jnp.stack([blocks, theirs])
+        upper = lax.axis_index(axis) >> level & 1
+        blocks = jnp.where(upper == 0, both, both[::-1]).reshape(-1, *value.shape)
+    return blocks
 
 
 def alternate(head_part, tail_part, groups):
@@ -23,7 +41,7 @@
     steps_count = query_rows // block_rows
     picked = jnp.take(corpus, sample_ids, axis=0)
     features_local = alternate(item_features, picked, groups)
-    gathered = lax.all_gather(features_local, "group", axis=1, tiled=True)
+    gathered = laid_out(doubled(features_local, "group"), 1)
     pre_act = jnp.dot(gathered, w1, preferred_element_type=jnp.float32)
     hidden = jnp.maximum(pre_act, 0.0).astype(jnp.bfloat16)
     partial_embed = jnp.dot(hidden, w2, preferred_element_type=jnp.float32)

time: 490 us -> 487 us (level)
  waiting for transfers between devices: 354 us -> 336 us
  local copies, waits for them, and re-layouts: 15.8 us -> 24.6 us
    all_gather x1 -> x0, waiting for transfers between devices: 71.4 us -> none  [per_device(): gathered = lax.all_gather(features_local, 'group', axis=1, tiled=True)]
    ppermute x0 -> x1, waiting for transfers between devices: none -> 52.8 us  [doubled(): theirs = lax.ppermute(blocks, axis, [(i, i ^ stride) for i in range(count)])]
    another operation x0 -> x2, local copies, waits for them, and re-layouts: none -> 8.77 us  [the longest x1 4.39 us: doubled(): both = jnp.stack([blocks, theirs])]
  transfers between devices with their start and end apart: 6 -> 6, of which waited for: 5 -> 5; matrix products, arithmetic and copies ran while one was open for 5% -> 6% of each run, Pallas kernels for 0% -> 0%
where the time goes in v1:
time: 487 us; the launch traced here: 486 us
  waiting for transfers between devices  336 us (69%)
  blocking collectives  44.2 us (9%)
  matrix products  40.8 us (8%)
  local copies, waits for them, and re-layouts  24.6 us (5%)
  other arithmetic  22.6 us (5%)
  between operations  13.9 us (3%)
    psum x1, waiting for transfers between devices, per_device(): grad_w1, grad_w2 = lax.psum((grad_w1, grad_w2), 'dp')  115 us
    reduce_scatter x1, waiting for transfers between devices, per_device(): grad_hat = lax.psum_scatter(grad_acc, 'dp', scatter_dimension=0, tiled=True)  109 us
    ppermute x1, waiting for transfers between devices, doubled(): theirs = lax.ppermute(blocks, axis, [(i, i ^ stride) for i in range(count)])  52.8 us
    all_gather x1, waiting for transfers between devices, per_device(): lax.all_gather(normed, 'dp', axis=0, tiled=True)  34.4 us
    reduce_scatter x1, waiting for transfers between devices, per_device(): lax.psum_scatter(partial_embed, 'group', scatter_dimension=0, tiled=True)  24.8 us
    all_gather x1, blocking collectives, per_device(): lax.all_gather(bias_own, 'dp', axis=0, tiled=True)  21.5 us
    all_gather x1, blocking collectives, per_device(): lax.all_gather(grad_embed.astype(jnp.bfloat16), 'group', axis=0, tiled=True)  12.8 us
  transfers between devices with their start and end apart: 6, of which 5 were waited for; matrix products, arithmetic and copies ran while one was open for 6% of the time, Pallas kernels for 0%

profile of v1, /device:TPU:0, one launch (start us, length us, event | category | flops | bytes accessed | tf_op | source)
XLA Modules:
  0.0 485.9 jit_solution(12874593888362967029)
XLA Ops:
  7.2 0.0 copy-start
  7.2 0.0 reduce-scatter.4.cloned.1.call-start
  7.2 0.8 fusion.9
  8.1 0.7 compare_and_fusion
  8.8 8.7 %gather_fusion = bf16[1024,1024]{1,0:T(8,128)(2,1)} fusion(bf16[2048,1024]{1,0:T(8,128)(2,1)} %param.9, s32[1024]{0:T(1024)S(1)} %fusion.9), kind=kCustom, calls=%fused_computation | custom fusion | bytes 4198400 | tf_op jit(solution)/shard_map/jit(_take)/gather | solution.py:42
  17.5 0.0 copy-start.6
  17.5 1.9 broadcast_select_fusion
  19.4 0.0 copy-done.6
  19.4 1.7 pad_maximum_fusion.1
  21.2 4.4 copy.16
  25.5 3.0 collective-permute-start
  28.5 4.4 copy.15
  32.9 52.8 %collective-permute-done = bf16[1,1280,1024]{1,2,0:T(8,128)(2,1)} collective-permute-done((bf16[1,1280,1024]{1,2,0:T(8,128)(2,1)}, bf16[1,1280,1024]{1,2,0:T(8,128)(2,1)}, u32[]{:S(2)}, u32[]{:S(2)}) %collective-permute-start) | collective-permute-done | bytes 2621472 | tf_op jit(solution)/shard_map/ppermute | solution.py:18
  85.7 3.0 pad_maximum_fusion
  88.7 1.0 reverse_select_fusion
  89.7 0.0 copy-start.4
  89.7 0.0 copy-done
  89.7 0.0 copy-start.8
  89.7 2.9 fusion.14
  92.7 0.0 copy-done.4
  92.7 0.0 copy-start.3
  92.7 1.5 copy-done.3
  94.1 0.0 copy-done.8
  94.1 0.0 copy-start.9
  94.1 1.6 fusion.6
  95.7 0.0 reduce-scatter.4.cloned.1.call-update
  95.7 0.0 all-gather.3.cloned.1.call-start
  95.8 24.8 %reduce-scatter.4.cloned.1.call-done = f32[640,256]{1,0:T(8,128)} async-done(((f32[1280,256]{1,0:T(8,128)}), f32[640,256]{1,0:T(8,128)}) %reduce-scatter.4.cloned.1.call-update) | async-done | bytes 655376 | tf_op jit(solution)/shard_map/reduce_scatter | solution.py:48
  120.6 1.3 multiply_reduce_fusion.1
  121.8 2.0 multiply_convert_fusion
  123.8 0.0 all-gather.3.cloned.1.call-update
  123.8 0.0 reduce-scatter.8.cloned.1.call-start
  123.9 0.0 copy-done.9
  123.9 0.1 dynamic-slice_negate_fusion
  124.0 21.5 %all-gather = bf16[16,1,640]{2,1,0:T(2,128)(2,1)S(1)} all-gather(bf16[1,1,640]{2,1,0:T(2,128)(2,1)S(1)} %reshape.72), channel_id=1, replica_groups=mesh['dp'=16,'group'=2] {'dp'}, dimensions={0}, use_global_device_ids=true | all-gather | bytes 21760 | tf_op jit(solution)/shard_map/all_gather | solution.py:55
  145.6 34.4 %all-gather.3.cloned.1.call-done = bf16[10240,256]{1,0:T(8,128)(2,1)} async-done(((bf16[640,256]{1,0:T(8,128)(2,1)}), bf16[10240,256]{1,0:T(8,128)(2,1)}) %all-gather.3.cloned.1.call-update) | async-done | bytes 5242896 | tf_op jit(solution)/shard_map/all_gather | solution.py:54
  180.0 0.0 copy-done.5
  180.0 6.6 %fusion.13 = (f32[256]{0:T(256)S(1)}, f32[10240,256]{1,0:T(8,128)}) fusion(f32[10240]{0:T(1024)S(1)} %bitcast.28, bf16[10240,256]{1,0:T(8,128)(2,1)} %all-gather.3.cloned.1.call-done, bf16[256,256]{1,0:T(8,128)(2,1)S(1)} %copy-done.5), kind=kOutput, calls=%fused_computation.40 | convolution fusion | flops 1350041344 | bytes 15901696 | tf_op jit(solution)/shard_map/while/body/eval_jaxpr/qe,ce->qc/dot_general | solution.py:63
  186.7 4.9 %pmax.7 = f32[256]{0:T(256)S(1)} all-reduce(f32[256]{0:T(256)S(1)} %get-tuple-element.43), channel_id=1, replica_groups=mesh['dp'=16,'group'=2] {'group'}, use_global_device_ids=true, to_apply=%region_3.4 | all-reduce | flops 256 | bytes 2048 | tf_op jit(solution)/shard_map/pmax | solution.py:75
  191.6 5.2 %exponential_reduce_fusion = f32[256]{0:T(256)S(1)} fusion(f32[10240,256]{1,0:T(8,128)} %get-tuple-element.44, f32[256]{0:T(256)S(1)} %get-tuple-element.43), kind=kLoop, calls=%fused_computation.4 | loop fusion | flops 5242624 | bytes 10487808 | tf_op jit(solution)/shard_map/while/body/eval_jaxpr/reduce_sum | solution.py:70
  196.8 4.9 %psum.21 = f32[256]{0:T(256)S(1)} all-reduce(f32[256]{0:T(256)S(1)} %exponential_multiply_fusion), channel_id=1, replica_groups=mesh['dp'=16,'group'=2] {'group'}, use_global_device_ids=true, to_apply=%region_5.6 | all-reduce | flops 256 | bytes 2048 | tf_op jit(solution)/shard_map/psum | solution.py:76
  201.7 9.5 %fusion.3 = f32[10240,256]{1,0:T(8,128)} fusion(bf16[256,256]{1,0:T(8,128)(2,1)S(1)} %copy-done.5, f32[10240,256]{1,0:T(8,128)} %get-tuple-element.44, f32[256]{0:T(256)S(1)} %log_add_fusion), kind=kOutput, calls=%fused_computation.13 | convolution fusion | flops 1347420160 | bytes 21103616 | tf_op jit(solution)/shard_map/while/body/eval_jaxpr/qc,qe->ce/dot_general | solution.py:91
  211.2 0.0 reduce-scatter.8.cloned.1.call-update
  211.2 0.2 reduce-scatter.6.cloned.1.call-start
  211.5 0.0 copy-start.2
  211.5 8.4 %fusion.2 = f32[256,256]{1,0:T(8,128)} fusion(bf16[10240,256]{1,0:T(8,128)(2,1)} %all-gather.3.cloned.1.call-done, f32[10240,256]{1,0:T(8,128)} %get-tuple-element.44, f32[256]{0:T(256)S(1)} %log_add_fusion), kind=kOutput, calls=%fused_computation.12 | convolution fusion | flops 1347420160 | bytes 15991808 | tf_op jit(solution)/shard_map/while/body/eval_jaxpr/dot_general | solution.py:94
  219.9 0.0 reduce-scatter.6.cloned.1.call-update
  219.9 0.0 all-reduce.5.cloned.1.call-start
  220.0 109.0 %reduce-scatter.8.cloned.1.call-done = f32[640,256]{1,0:T(8,128)} async-done(((f32[10240,256]{1,0:T(8,128)}), f32[640,256]{1,0:T(8,128)}) %reduce-scatter.8.cloned.1.call-update) | async-done | bytes 655376 | tf_op jit(solution)/shard_map/reduce_scatter | solution.py:99
  329.0 0.0 copy-done.2
  329.0 1.3 multiply_reduce_fusion
  330.3 1.4 subtract_convert_fusion
  331.7 12.8 %all_gather.11 = bf16[1280,256]{1,0:T(8,128)(2,1)S(1)} all-gather(bf16[640,256]{1,0:T(8,128)(2,1)S(1)} %subtract_convert_fusion), channel_id=1, replica_groups=mesh['dp'=16,'group'=2] {'group'}, dimensions={0}, use_global_device_ids=true | all-gather | bytes 983040 | tf_op jit(solution)/shard_map/all_gather | solution.py:110
  344.5 8.6 %fusion.4 = f32[2048,512]{1,0:T(8,128)} fusion(bf16[1280,2048]{0,1:T(8,128)(2,1)} %bitcast.26, bf16[1280,256]{1,0:T(8,128)(2,1)S(1)} %all_gather.11, bf16[512,256]{1,0:T(8,128)(2,1)S(1)} %copy-done.8, f32[1280,512]{1,0:T(8,128)} %copy-done.3), kind=kOutput, calls=%fused_computation.14 | convolution fusion | flops 3021864960 | bytes 12976128 | tf_op jit(solution)/shard_map/rf,rh->fh/dot_general | solution.py:115
  353.2 3.1 fusion.5
  356.3 0.0 all-reduce.5.cloned.1.call-update
  356.3 0.0 reduce-scatter.6.cloned.1.call-done
  356.3 1.6 fusion.8
  357.9 0.6 multiply_subtract_fusion
  358.5 115.3 %all-reduce.5.cloned.1.call-done = (f32[2048,512]{1,0:T(8,128)}, f32[512,256]{1,0:T(8,128)}) async-done(((f32[2048,512]{1,0:T(8,128)}, f32[512,256]{1,0:T(8,128)}), (f32[2048,512]{1,0:T(8,128)}, f32[512,256]{1,0:T(8,128)})) %all-reduce.5.cloned.1.call-update) | async-done | bytes 4718608 | tf_op jit(solution)/shard_map/psum | solution.py:116
  473.8 4.8 copy.19
  478.6 0.0 copy-done.7
  478.6 0.8 copy.20
  479.4 0.0 copy-done.1
  (11 shorter events, 0.1 us)
Async XLA Ops:
  7.2 82.5 %copy-start = (bf16[2048,512]{1,0:T(8,128)(2,1)S(1)}, bf16[2048,512]{1,0:T(8,128)(2,1)}, u32[]{:S(2)}) copy-start(bf16[2048,512]{1,0:T(8,128)(2,1)} %param.12) | copy-start | bytes 6291460
  7.2 113.4 %reduce-scatter.4.cloned.1.call-start = ((), (), s32[]{:S(2)}) async-start(), calls=%async_computation.3 | async-start | bytes 1966080 | tf_op jit(solution)/shard_map/reduce_scatter | solution.py:48
  17.5 1.9 copy-start.6
  25.5 60.1 %collective-permute-start = (bf16[1,1280,1024]{1,2,0:T(8,128)(2,1)}, bf16[1,1280,1024]{1,2,0:T(8,128)(2,1)}, u32[]{:S(2)}, u32[]{:S(2)}) collective-permute-start(bf16[1,1280,1024]{1,2,0:T(8,128)(2,1)} %copy.16), channel_id=1, source_target_pairs={{0,1},{1,0},{2,3},{3,2},{4,5},{5,4},{6,7},{7,6},{8,9},{9,8},{10,11... | collective-permute-start | bytes 7864328 | tf_op jit(solution)/shard_map/ppermute | solution.py:18
  89.7 3.0 copy-start.4
  89.7 4.4 copy-start.8
  92.7 1.5 copy-start.3
  94.1 29.7 %copy-start.9 = (bf16[1024]{0:T(1024)(128)(2,1)S(1)}, bf16[1024]{0:T(1024)(128)(2,1)}, u32[]{:S(2)}) copy-start(bf16[1024]{0:T(1024)(128)(2,1)} %param.11) | copy-start | bytes 6148
  94.1 85.9 %copy-start.5 = (bf16[256,256]{1,0:T(8,128)(2,1)S(1)}, bf16[256,256]{1,0:T(8,128)(2,1)}, u32[]{:S(2)}) copy-start(bf16[256,256]{1,0:T(8,128)(2,1)} %param.7) | copy-start | bytes 393220
  95.7 84.3 %all-gather.3.cloned.1.call-start = ((), (), s32[]{:S(2)}) async-start(), calls=%async_computation.4 | async-start | bytes 5570560 | tf_op jit(solution)/shard_map/all_gather | solution.py:54
  123.8 205.2 %reduce-scatter.8.cloned.1.call-start = ((), (), s32[]{:S(2)}) async-start(), calls=%async_computation.6 | async-start | bytes 11141120 | tf_op jit(solution)/shard_map/reduce_scatter | solution.py:99
  211.2 145.1 %reduce-scatter.6.cloned.1.call-start = ((), (), s32[]{:S(2)}) async-start(), calls=%async_computation.5 | async-start | bytes 393216 | tf_op jit(solution)/shard_map/reduce_scatter | solution.py:100
  211.5 117.5 %copy-start.2 = (f32[640,256]{1,0:T(8,128)S(1)}, f32[640,256]{1,0:T(8,128)}, u32[]{:S(2)}) copy-start(f32[640,256]{1,0:T(8,128)} %reduce-scatter.4.cloned.1.call-done) | copy-start | bytes 1966084
  219.9 253.8 %all-reduce.5.cloned.1.call-start = ((), (), s32[]{:S(2)}) async-start(), calls=%async_computation.7 | async-start | bytes 9437184 | tf_op jit(solution)/shard_map/psum | solution.py:116
  473.8 5.6 %copy-start.1 = (bf16[2048,512]{1,0:T(8,128)(2,1)S(1)}, bf16[2048,512]{1,0:T(8,128)(2,1)}, u32[]{:S(2)}) copy-start(bf16[2048,512]{1,0:T(8,128)(2,1)} %param.12) | copy-start | bytes 6291460
  473.8 4.8 copy-start.7
Sparse Core Ops, SparseCore 0:
  95.8 24.6 reduce-scatter.3
  123.9 56.0 all-gather.2
  211.4 117.6 reduce-scatter.7
  331.2 13.6 reduce-scatter.5
  356.4 117.3 all-reduce.4
